TPU v7x, 1024 devices: a whole 4x8x16 slice. The times are simulated.
1024 devices in a mesh: dp: 4 (over x_hi, core), mp: 256 (over z, x_lo, y).
Axes of the slice: x: 4 (x_hi: 2, x_lo: 2; x = x_hi * 2 + x_lo), y: 8, z: 16, core: 2. Of those that a mesh axis runs over, the one named last changes fastest.
Arguments:
- block_input: bfloat16 [768, 6144], P('dp'), may hold values from -6 to 6
- grad_out: bfloat16 [768, 6144], P('dp'), may hold values from -6 to 6
- ln_gain: float32 [6144], replicated, may hold values from 0.1 to 1.9
- w_in: bfloat16 [6144, 24576], P(None, 'mp'), may hold values from -0.078125 to 0.078125
- w_out: bfloat16 [24576, 6144], P('mp'), may hold values from -0.0390625 to 0.0390625
Outputs:
- grad_input: bfloat16 [768, 6144], P('dp', 'mp')
- grad_w_in: float32 [6144, 24576], P('dp', 'mp')
- grad_w_out: float32 [24576, 6144], P('mp', 'dp')
All inputs are finite; a program needn't handle non-finite values.
Results may differ from a plain program's by a relative error of at most 0.0055.
Values may be sent and summed in bfloat16 or wider, within the bound.
A program may use at most 64 MiB of HBM per device.

v0:
```python
import jax
import jax.numpy as jnp
from jax import lax
from jax.sharding import PartitionSpec as P


def gelu_slope(pre_gelu):
    normal_cdf = 0.5 * (1.0 + lax.erf(pre_gelu * 0.7071067811865476))
    return normal_cdf + pre_gelu * jnp.exp(-0.5 * pre_gelu * pre_gelu) * 0.3989422804014327


def contract_rows(left_mat, right_mat):
    return lax.dot_general(
        left_mat, right_mat, (((0,), (0,)), ((), ())), preferred_element_type=jnp.float32
    )


def contract_cols(left_mat, right_mat):
    return lax.dot_general(
        left_mat, right_mat, (((1,), (1,)), ((), ())), preferred_element_type=jnp.float32
    )


def shards(block_input, grad_out, ln_gain, w_in, w_out):
    input_float = block_input.astype(jnp.float32)
    centred = input_float - jnp.mean(input_float, axis=1, keepdims=True)
    inv_std = lax.rsqrt(jnp.mean(centred * centred, axis=1, keepdims=True) + 1e-06)
    normed = centred * inv_std
    gain_normed = (normed * ln_gain).astype(jnp.bfloat16)
    pre_gelu = jnp.dot(gain_normed, w_in, preferred_element_type=jnp.float32)
    activation = jax.nn.gelu(pre_gelu, approximate=False).astype(jnp.bfloat16)
    grad_act = contract_cols(grad_out, w_out)
    grad_pre = (grad_act * gelu_slope(pre_gelu)).astype(jnp.bfloat16)
    grad_w_out = lax.psum_scatter(
        contract_rows(activation, grad_out), "dp", scatter_dimension=1, tiled=True
    )
    grad_w_in = lax.psum_scatter(
        contract_rows(gain_normed, grad_pre), "dp", scatter_dimension=0, tiled=True
    )
    features = ln_gain.shape[0]
    col_width = features // lax.axis_size("mp")
    offset = lax.axis_index("mp") * col_width
    normed_cols = lax.dynamic_slice_in_dim(normed, offset, col_width, 1)
    gain_cols = lax.dynamic_slice_in_dim(ln_gain, offset, col_width, 0)
    grad_cols = lax.dynamic_slice_in_dim(grad_out, offset, col_width, 1).astype(jnp.float32)
    grad_rows = lax.psum_scatter(
        contract_cols(w_in, grad_pre), "mp", scatter_dimension=0, tiled=True
    )
    grad_normed = jnp.transpose(grad_rows) * gain_cols
    total_one, total_two = lax.psum(
        (jnp.sum(grad_normed, axis=1), jnp.sum(grad_normed * normed_cols, axis=1)), "mp"
    )
    mean_one = (total_one / features)[:, None]
    mean_two = (total_two / features)[:, None]
    grad_input = (grad_cols + inv_std * (grad_normed - mean_one - normed_cols * mean_two)).astype(
        jnp.bfloat16
    )
    return (grad_input, grad_w_in, grad_w_out)


def solution(mesh):
    in_specs = (P("dp", None), P("dp", None), P(), P(None, "mp"), P("mp", None))
    out_specs = (P("dp", "mp"), P("dp", "mp"), P("mp", "dp"))
    return jax.shard_map(shards, mesh=mesh, in_specs=in_specs, out_specs=out_specs, check_vma=False)
```

profile of v0, /device:TPU:4, one launch (start us, length us, event | category | flops | bytes accessed | tf_op | source)
XLA Modules:
  0.0 1892.7 jit_solution(12477183764603698802)
XLA Ops:
  7.2 0.0 copy-start
  7.2 0.0 copy-start.1
  7.2 0.0 reduce-scatter.10.cloned.1.call-start
  7.2 0.0 copy-start.6
  7.2 2.2 convert_reduce_fusion
  9.5 0.2 copy-done.1
  9.7 0.8 fusion.2
  10.4 0.0 copy-done
  10.4 0.0 copy-done.6
  10.4 0.0 copy-start.2
  10.5 0.0 copy-start.3
  10.5 0.9 fusion.5
  11.4 0.7 copy-done.2
  12.1 0.3 copy-done.3
  12.4 0.0 copy-start.4
  12.4 0.8 fusion.3
  13.2 0.0 copy-done.4
  13.2 0.0 copy-start.5
  13.2 0.6 copy-done.5
  13.8 3.0 convolution_bitcast_fusion
  16.8 6.2 copy.10
  23.0 0.0 reduce-scatter.10.cloned.1.call-update
  23.1 0.0 reduce-scatter.6.cloned.1.call-start
  23.1 3.3 fusion.4
  26.4 0.0 reduce-scatter.6.cloned.1.call-update
  26.5 0.0 reduce-scatter.8.cloned.1.call-start
  26.5 3.8 fusion.25
  30.3 0.0 reduce-scatter.8.cloned.1.call-update
  30.4 0.8 dynamic_slice.10
  31.1 3.0 fusion
  34.2 1240.8 %reduce-scatter.10.cloned.1.call-done = f32[24,192]{1,0:T(8,128)} async-done(((f32[6144,192]{1,0:T(8,128)}), f32[24,192]{1,0:T(8,128)}) %reduce-scatter.10.cloned.1.call-update) | async-done | bytes 18448
  1274.9 0.8 copy.11
  1275.8 0.1 multiply_reduce_fusion
  1275.9 1.1 fusion.17
  1277.0 607.3 %all-reduce = (f32[192]{0:T(256)S(1)}, f32[192]{0:T(256)S(1)}) all-reduce(f32[192]{0:T(256)S(1)} %fusion.17, f32[192]{0:T(256)S(1)} %multiply_reduce_fusion), channel_id=1, replica_groups=mesh['dp'=4,'mp'=256] {'mp'}, use_global_device_ids=true, to_apply=%region_6.0 | all-reduce | flops 384 | bytes 3072 | tf_op jit(solution)/shard_map/psum | solution.py:50
  1884.3 1.2 fusion.16
  1885.5 0.7 copy.9
  1886.1 0.0 reduce-scatter.6.cloned.1.call-done
  1886.1 0.0 reduce-scatter.8.cloned.1.call-done
  (3 shorter events, 0.0 us)
Async XLA Ops:
  7.2 3.3 copy-start
  7.2 2.5 copy-start.1
  7.2 1267.7 %reduce-scatter.10.cloned.1.call-start = ((), (), s32[]{:S(2)}) async-start(), calls=%async_computation.5 | async-start | bytes 6316032
  7.2 3.2 copy-start.6
  10.4 1.7 copy-start.2
  10.5 2.0 copy-start.3
  12.4 0.8 copy-start.4
  13.2 0.6 copy-start.5
  23.1 1863.1 %reduce-scatter.6.cloned.1.call-start = ((), (), s32[]{:S(2)}) async-start(), calls=%async_computation.3 | async-start | bytes 2949120 | tf_op jit(solution)/shard_map/reduce_scatter | solution.py:37
  26.5 1859.7 %reduce-scatter.8.cloned.1.call-start = ((), (), s32[]{:S(2)}) async-start(), calls=%async_computation.4 | async-start | bytes 2949120 | tf_op jit(solution)/shard_map/reduce_scatter | solution.py:34
Sparse Core Ops, SparseCore 0:
  23.2 1251.6 reduce-scatter.9
  1279.6 52.0 reduce-scatter.5
  1335.9 61.2 reduce-scatter.7
where the time goes:
time: 1890 us
  waiting for transfers between devices  1240 us (66%)
  blocking collectives  607 us (32%)
    unnamed x4, waiting for transfers between devices  1240 us
    psum x1, blocking collectives, shards(): lax.psum((jnp.sum(grad_normed, axis=1), jnp.sum(grad_normed * normed_cols...  607 us
  transfers between devices with their start and end apart: 3, of which 1 were waited for; matrix products, arithmetic and copies ran while one was open for 1% of the time, Pallas kernels for 0%

commit v1 on v0

v1 whole, which is shorter than its diff:
```python
import jax
import jax.numpy as jnp
from jax import lax
from jax.experimental import pallas as pl
from jax.experimental.pallas import tpu as pltpu
from jax.sharding import PartitionSpec as P

F32 = jnp.float32
BF16 = jnp.bfloat16
D = 6144
TOK = 192
HID = 96
LANE = 128
NY = 8
NZ = 16
YCOL = D // NY
XCOL = YCOL // 2
PIECE = XCOL // NZ
QUART = D // 4
XROWS = 48


def contract_last(left, right):
    return lax.dot_general(left, right, (((1,), (1,)), ((), ())), preferred_element_type=F32)


def remote(src, dst, send, recv, dp, mp):
    return pltpu.make_async_remote_copy(
        src_ref=src,
        dst_ref=dst,
        send_sem=send,
        recv_sem=recv,
        device_id=(dp, mp),
        device_id_type=pl.DeviceIdType.MESH,
    )


def hi_lo(value):
    high = value.astype(BF16).astype(F32)
    return high, (value - high).astype(BF16).astype(F32)


def kernel(
    x_hbm, go_hbm, gain_ref, win_hbm, wout_hbm,
    gi_ref, gwin_ref, gwout_ref,
    x_v, go_v, g_v, win_v, wout_v, wg, gpg, gain3, pre_s, ga_s, u_s, stat_s, tr_s, gp_t, act_t,
    pair_send, pair_recv, xh_send, xh_recv, gg_s, gg_t, xl_send, xl_recv, st_t, xst_send, xst_recv,
    z_send, z_recv, last_send, last_recv,
    x_sem, load_sem, a_send, a_recv, f_send, f_recv, y_send, y_recv, p_send, p_recv,
    h_send, h_recv, l_send, l_recv, s_send, s_recv, zs_sem, zr_sem, e_send, e_recv,
):
    dp = lax.axis_index("dp")
    mp = lax.axis_index("mp")
    xh, core = dp // 2, dp % 2
    z, xl, y = mp // 16, (mp // 8) % 2, mp % 8
    pair = 2 * xh + (1 - core)
    far = 2 * (1 - xh) + core
    xl_mp = z * 16 + (1 - xl) * 8 + y
    to_mp = (2 * y + xl) * 16 + (z // 8) * 8 + z % 8
    from_mp = (8 * xl + y) * 16 + (z % 2) * 8 + z // 2

    def y_mp(other):
        return z * 16 + xl * 8 + other

    def z_mp(other):
        return other * 16 + xl * 8 + y

    x_loads = [
        pltpu.make_async_copy(
            x_hbm.at[pl.ds(i * XROWS, XROWS)], x_v.at[pl.ds(i * XROWS, XROWS)], x_sem.at[i]
        )
        for i in range(TOK // XROWS)
    ]
    win_load = pltpu.make_async_copy(win_hbm, win_v.at[pl.ds(0, HID)], load_sem.at[0])
    wout_load = pltpu.make_async_copy(wout_hbm, wout_v.at[pl.ds(0, HID)], load_sem.at[1])
    go_load = pltpu.make_async_copy(go_hbm, go_v, load_sem.at[2])
    own_cols = pl.ds(pl.multiple_of(y * YCOL, YCOL), YCOL)
    own_load = pltpu.make_async_copy(
        win_hbm.at[:, own_cols],
        wg.at[pl.ds(pl.multiple_of(y * LANE, LANE), HID)],
        load_sem.at[3],
    )
    for load in x_loads:
        load.start()
    win_load.start()
    wout_load.start()
    go_load.start()
    own_load.start()

    barrier = pltpu.get_barrier_semaphore()

    def greet(to_dp, to_mp_):
        pl.semaphore_signal(
            barrier, inc=1, device_id=(to_dp, to_mp_), device_id_type=pl.DeviceIdType.MESH
        )

    @pl.loop(1, NY)
    def _(d):
        greet(dp, y_mp((y + d) % NY))

    @pl.loop(1, NZ)
    def _(d):
        greet(dp, z_mp((z + d) % NZ))

    greet(pair, mp)
    greet(far, mp)
    greet(dp, xl_mp)
    moves = to_mp != mp

    @pl.when(moves)
    def _():
        greet(dp, to_mp)
        greet(dp, from_mp)

    pl.semaphore_wait(barrier, NY - 1 + NZ - 1 + 3 + jnp.where(moves, 2, 0))

    def block_copy(d):
        other = (y + d) % NY
        return remote(
            win_hbm.at[pl.ds(pl.multiple_of(core * 48, 16), 48), pl.ds(pl.multiple_of(other * YCOL, YCOL), YCOL)],
            wg.at[pl.ds(pl.multiple_of(y * LANE + core * 48, 16), 48)],
            a_send.at[d], a_recv.at[d], dp, y_mp(other),
        )

    def block_landed(d):
        source = (y + NY - d) % NY
        return wg.at[pl.ds(pl.multiple_of(source * LANE + core * 48, 16), 48)]

    def block_arrival(d):
        landed = block_landed(d)
        return remote(landed, landed, a_send.at[d], a_recv.at[d], dp, y_mp((y + d) % NY))

    def forward(d):
        landed = block_landed(d)
        return remote(landed, landed, f_send.at[d], f_recv.at[d], pair, mp)

    def forward_arrival(d):
        source = (y + NY - d) % NY
        landed = wg.at[pl.ds(pl.multiple_of(source * LANE + (1 - core) * 48, 16), 48)]
        return remote(landed, landed, f_send.at[d], f_recv.at[d], pair, mp)

    @pl.loop(1, NY)
    def _(d):
        block_copy(d).start()

    for i in range(NY):
        wg[i * LANE + HID : (i + 1) * LANE, :] = jnp.zeros((LANE - HID, YCOL), BF16)
    win_v[HID:, :] = jnp.zeros((LANE - HID, D), BF16)
    wout_v[HID:, :] = jnp.zeros((LANE - HID, D), BF16)

    lane = lax.broadcasted_iota(jnp.int32, (16, LANE), 1)
    for i in range(TOK // XROWS):
        x_loads[i].wait()

        @pl.loop(0, XROWS // 16)
        def _(t):
            rows = pl.ds(pl.multiple_of(i * XROWS + t * 16, 16), 16)
            tile = x_v[rows, :].astype(F32)
            mean = jnp.sum(tile, axis=1, keepdims=True) * (1.0 / D)
            centred = tile - mean
            inv = lax.rsqrt(jnp.sum(centred * centred, axis=1, keepdims=True) * (1.0 / D) + 1e-06)
            g_v[rows, :] = (centred * inv * gain_ref[...]).astype(BF16)
            stat_s[rows, :] = jnp.where(lane < 64, mean, inv)

    gain = gain_ref[...]
    g_hi = gain.astype(BF16).astype(F32)
    g_mid = (gain - g_hi).astype(BF16).astype(F32)
    g_low = gain - g_hi - g_mid
    row = lax.broadcasted_iota(jnp.int32, (16, D), 0)
    gain3[...] = jnp.where(
        row == 0, g_hi, jnp.where(row == 1, g_mid, jnp.where(row == 2, g_low, 0.0))
    ).astype(BF16)

    win_load.wait()
    wout_load.wait()
    go_load.wait()
    pre_s[...] = jnp.zeros_like(pre_s)
    ga_s[...] = jnp.zeros_like(ga_s)
    u_s[...] = jnp.zeros_like(u_s)

    @pl.loop(0, 4)
    def _(k):
        part = pl.ds(pl.multiple_of(k * 1536, 1536), 1536)
        w_part = win_v[:, part]
        pre_s[...] += contract_last(g_v[:, part], w_part)
        u_s[...] += contract_last(gain3[:, part], w_part)
        ga_s[...] += contract_last(go_v[:, part], wout_v[:, part])

    pre = pre_s[...]
    cdf = 0.5 * (1.0 + lax.erf(pre * 0.7071067811865476))
    act = (pre * cdf).astype(BF16).astype(F32)
    slope = cdf + pre * jnp.exp(-0.5 * pre * pre) * 0.3989422804014327
    gp = (ga_s[...] * slope).astype(BF16).astype(F32)
    u_row = jnp.sum(u_s[...], axis=0, keepdims=True)
    one_hi, one_lo = hi_lo(jnp.sum(gp * u_row, axis=1, keepdims=True))
    two_hi, two_lo = hi_lo(jnp.sum(gp * pre, axis=1, keepdims=True))
    lanes = lax.broadcasted_iota(jnp.int32, (TOK, LANE), 1)
    tail = jnp.where(lanes == HID, one_hi, 0.0)
    tail = jnp.where(lanes == HID + 1, one_lo, tail)
    tail = jnp.where(lanes == HID + 2, two_hi, tail)
    tail = jnp.where(lanes == HID + 3, two_lo, tail)
    own_block = pl.ds(pl.multiple_of(y * LANE, LANE), LANE)
    gpg[:, own_block] = (gp + tail).astype(BF16)

    def gather_copy(d):
        mine = gpg.at[:, own_block]
        return remote(mine, mine, y_send.at[d], y_recv.at[d], dp, y_mp((y + d) % NY))

    def gather_arrival(d):
        source = (y + NY - d) % NY
        landed = gpg.at[:, pl.ds(pl.multiple_of(source * LANE, LANE), LANE)]
        return remote(landed, landed, y_send.at[d], y_recv.at[d], dp, y_mp((y + d) % NY))

    @pl.loop(1, NY)
    def _(d):
        gather_copy(d).start()

    tr_s[TOK:, :] = jnp.zeros((256 - TOK, LANE), F32)
    for values, target in ((gp, gp_t), (act, act_t)):
        tr_s[:TOK, :] = values
        for b in range(2):
            target[:, b * 128 : (b + 1) * 128] = tr_s[b * 128 : (b + 1) * 128, :].T.astype(BF16)
    sides = ((gp_t, g_v, gwin_ref), (act_t, go_v, gwout_ref))

    def product(side, quarter, t):
        left, right, _ = sides[side]
        cols = pl.ds(pl.multiple_of(quarter * QUART + t * 768, 128), 768)
        return jnp.dot(left[:HID, :TOK], right[:, cols], preferred_element_type=F32)

    def pair_copy(r):
        return remote(pair_send.at[r], pair_recv.at[r], p_send.at[r], p_recv.at[r], pair, mp)

    for r in range(2):
        half = 1 - xh if r == 0 else xh
        for side in range(2):
            for t in range(2):
                pair_send[r, side, :, t * 768 : (t + 1) * 768] = product(
                    side, 2 * half + 1 - core, t
                ).astype(BF16)
        pair_copy(r).start()

    @pl.loop(1, NY)
    def _(d):
        block_arrival(d).wait_recv()
        forward(d).start()

    for side in range(2):
        for t in range(2):
            sides[side][2][:, t * 768 : (t + 1) * 768] = product(side, dp, t)

    pair_copy(0).wait_recv()
    for side in range(2):
        for t in range(2):
            cols = slice(t * 768, (t + 1) * 768)
            xh_send[side, :, cols] = (
                product(side, far, t) + pair_recv[0, side, :, cols].astype(F32)
            ).astype(BF16)
    far_copy = remote(xh_send, xh_recv, h_send, h_recv, far, mp)
    far_copy.start()

    own_load.wait()

    @pl.loop(1, NY)
    def _(d):
        gather_arrival(d).wait_recv()
        forward_arrival(d).wait_recv()

    packed = jnp.zeros((TOK, LANE), F32)
    for i in range(NY):
        packed += gpg[:, i * LANE : (i + 1) * LANE].astype(F32)
    tr_s[:TOK, :] = packed
    for b in range(2):
        st_t[:, b * 128 : (b + 1) * 128] = tr_s[b * 128 : (b + 1) * 128, :].T
    xst_send[...] = st_t[HID : HID + 8, :]
    stat_copy = remote(xst_send, xst_recv, s_send, s_recv, dp, xl_mp)
    stat_copy.start()

    def hidden_sum(which):
        cols = pl.ds(pl.multiple_of(which * XCOL, XCOL), XCOL)
        return jnp.dot(gpg[...], wg[:, cols], preferred_element_type=F32)

    xl_send[...] = hidden_sum(1 - xl).astype(BF16)
    half_copy = remote(xl_send, xl_recv, l_send, l_recv, dp, xl_mp)
    half_copy.start()
    gg_s[TOK:, :] = jnp.zeros((256 - TOK, XCOL), F32)
    gg_s[:TOK, :] = hidden_sum(xl)

    half_copy.wait_recv()
    gg_s[:TOK, :] += xl_recv[...].astype(F32)
    for c in range(XCOL // 128):
        for b in range(2):
            gg_t[c * 128 : (c + 1) * 128, b * 128 : (b + 1) * 128] = gg_s[
                b * 128 : (b + 1) * 128, c * 128 : (c + 1) * 128
            ].T
    stat_copy.wait_recv()
    stats = xst_send[...] + xst_recv[...]
    one_hi, one_lo = hi_lo(stats[0:1] + stats[1:2])
    two_hi, two_lo = hi_lo(stats[2:3] + stats[3:4])
    sub = lax.broadcasted_iota(jnp.int32, (8, 256), 0)
    tail8 = jnp.where(sub == 0, one_hi, 0.0)
    tail8 = jnp.where(sub == 1, one_lo, tail8)
    tail8 = jnp.where(sub == 2, two_hi, tail8)
    tail8 = jnp.where(sub == 3, two_lo, tail8)

    def piece_copy(d):
        return remote(z_send.at[d], z_recv.at[d], zs_sem.at[d], zr_sem.at[d], dp, z_mp((z + d) % NZ))

    def piece(place):
        return jnp.concatenate(
            [gg_t[pl.ds(pl.multiple_of(place * PIECE, 8), PIECE), :], tail8], axis=0
        )

    @pl.loop(1, NZ)
    def _(d):
        z_send[d] = piece((z + d) % NZ).astype(BF16)
        piece_copy(d).start()

    last_send[...] = piece(z)

    @pl.loop(1, NZ)
    def _(d):
        piece_copy(d).wait_recv()
        last_send[...] += z_recv[d].astype(F32)

    last_copy = remote(last_send, last_recv, e_send, e_recv, dp, to_mp)

    @pl.when(moves)
    def _():
        last_copy.start()

    @pl.when(to_mp == mp)
    def _():
        last_recv[...] = last_send[...]

    pair_copy(1).wait_recv()
    far_copy.wait_recv()
    for side in range(2):
        out = sides[side][2]
        out[...] += pair_recv[1, side].astype(F32) + xh_recv[side].astype(F32)

    base = pl.multiple_of(jnp.minimum((mp * PIECE) // 128 * 128, D - 256), 128)
    off = mp * PIECE - base
    span = pl.ds(base, 256)
    picks = lax.broadcasted_iota(jnp.int32, (32, 256), 1) == (
        lax.broadcasted_iota(jnp.int32, (32, 256), 0) + off
    )
    pick = jnp.where(picks, 1.0, 0.0)
    x_t = contract_last(pick.astype(BF16), x_v[:, span])[:PIECE]
    go_t = contract_last(pick.astype(BF16), go_v[:, span])[:PIECE]
    gain_t = jnp.sum(pick * gain_ref[:, span], axis=1, keepdims=True)[:PIECE]
    stat_s[TOK:, :] = jnp.zeros((256 - TOK, LANE), F32)
    for b in range(2):
        st_t[:, b * 128 : (b + 1) * 128] = stat_s[b * 128 : (b + 1) * 128, :].T
    mean_row, inv_row = st_t[0:1, :TOK], st_t[64:65, :TOK]
    normed = (x_t - mean_row) * inv_row
    full = last_send[PIECE:, :TOK]
    mean_one = (full[0:1] + full[1:2]) * (1.0 / D)
    mean_two = (full[2:3] + full[3:4]) * (1.0 / D)

    @pl.when(moves)
    def _():
        last_copy.wait_recv()

    grad_normed = last_recv[:PIECE, :TOK] * gain_t
    gi_ref[...] = (go_t + inv_row * (grad_normed - mean_one - normed * mean_two)).astype(BF16)

    @pl.loop(1, NY)
    def _(d):
        block_copy(d).wait_send()
        forward(d).wait_send()
        gather_copy(d).wait_send()

    for r in range(2):
        pair_copy(r).wait_send()
    far_copy.wait_send()
    stat_copy.wait_send()
    half_copy.wait_send()

    @pl.loop(1, NZ)
    def _(d):
        piece_copy(d).wait_send()

    @pl.when(moves)
    def _():
        last_copy.wait_send()


def shards(block_input, grad_out, ln_gain, w_in, w_out):
    dma = pltpu.SemaphoreType.DMA
    grad_input, grad_w_in, grad_w_out = pl.pallas_call(
        kernel,
        out_shape=(
            jax.ShapeDtypeStruct((PIECE, TOK), BF16),
            jax.ShapeDtypeStruct((HID, QUART), F32),
            jax.ShapeDtypeStruct((HID, QUART), F32),
        ),
        in_specs=[
            pl.BlockSpec(memory_space=pl.ANY),
            pl.BlockSpec(memory_space=pl.ANY),
            pl.BlockSpec(memory_space=pltpu.VMEM),
            pl.BlockSpec(memory_space=pl.ANY),
            pl.BlockSpec(memory_space=pl.ANY),
        ],
        out_specs=[pl.BlockSpec(memory_space=pltpu.VMEM)] * 3,
        scratch_shapes=[
            pltpu.VMEM((TOK, D), BF16),
            pltpu.VMEM((TOK, D), BF16),
            pltpu.VMEM((TOK, D), BF16),
            pltpu.VMEM((LANE, D), BF16),
            pltpu.VMEM((LANE, D), BF16),
            pltpu.VMEM((NY * LANE, YCOL), BF16),
            pltpu.VMEM((TOK, NY * LANE), BF16),
            pltpu.VMEM((16, D), BF16),
            pltpu.VMEM((TOK, LANE), F32),
            pltpu.VMEM((TOK, LANE), F32),
            pltpu.VMEM((16, LANE), F32),
            pltpu.VMEM((256, LANE), F32),
            pltpu.VMEM((256, LANE), F32),
            pltpu.VMEM((LANE, 256), BF16),
            pltpu.VMEM((LANE, 256), BF16),
            pltpu.VMEM((2, 2, HID, QUART), BF16),
            pltpu.VMEM((2, 2, HID, QUART), BF16),
            pltpu.VMEM((2, HID, QUART), BF16),
            pltpu.VMEM((2, HID, QUART), BF16),
            pltpu.VMEM((256, XCOL), F32),
            pltpu.VMEM((XCOL, 256), F32),
            pltpu.VMEM((TOK, XCOL), BF16),
            pltpu.VMEM((TOK, XCOL), BF16),
            pltpu.VMEM((LANE, 256), F32),
            pltpu.VMEM((8, 256), F32),
            pltpu.VMEM((8, 256), F32),
            pltpu.VMEM((NZ, 32, 256), BF16),
            pltpu.VMEM((NZ, 32, 256), BF16),
            pltpu.VMEM((32, 256), F32),
            pltpu.VMEM((32, 256), F32),
            dma((4,)), dma((4,)),
            dma((NY,)), dma((NY,)), dma((NY,)), dma((NY,)), dma((NY,)), dma((NY,)),
            dma((2,)), dma((2,)), dma, dma, dma, dma, dma, dma,
            dma((NZ,)), dma((NZ,)), dma, dma,
        ],
        compiler_params=pltpu.CompilerParams(
            collective_id=0, has_side_effects=True, vmem_limit_bytes=60 * 1024 * 1024
        ),
        cost_estimate=pl.CostEstimate(
            flops=2 * 5 * TOK * D * HID, bytes_accessed=9 * 1024 * 1024, transcendentals=TOK * HID
        ),
    )(block_input, grad_out, ln_gain.reshape(1, D), w_in.T, w_out)
    return grad_input.T, grad_w_in.T, grad_w_out


def solution(mesh):
    in_specs = (P("dp", None), P("dp", None), P(), P(None, "mp"), P("mp", None))
    out_specs = (P("dp", "mp"), P("dp", "mp"), P("mp", "dp"))
    return jax.shard_map(shards, mesh=mesh, in_specs=in_specs, out_specs=out_specs, check_vma=False)
```

time: 1890 us -> 83.4 us (0.04)
  the two profiles are of different devices: /device:TPU:4 before, /device:TPU:22 now
where the time goes in v1:
time: 83.4 us; the launch traced here: 83.1 us
  Pallas kernels  77.3 us (93%)
  local copies, waits for them, and re-layouts  5.14 us (6%)
    pallas_call x1, Pallas kernels, shards(): pl.pallas_call(kernel, out_shape=(jax.ShapeDtypeStruct((PIECE, TOK), BF16...  77.3 us
    unnamed x3, local copies, waits for them, and re-layouts  5.14 us

profile of v1, /device:TPU:22, one launch (start us, length us, event | category | flops | bytes accessed | tf_op | source)
XLA Modules:
  0.0 83.1 jit_solution(3279348511402126367)
XLA Ops:
  0.6 77.3 %shard_map.76 = (bf16[24,192]{1,0:T(8,128)(2,1)}, f32[96,1536]{1,0:T(8,128)}, f32[96,1536]{1,0:T(8,128)}) custom-call(bf16[192,6144]{1,0:T(8,128)(2,1)} %x_hbm.1, bf16[192,6144]{1,0:T(8,128)(2,1)} %go_hbm.1, f32[1,6144]{1,0:T(1,128)} %bitcast.6, bf16[96,6144]{1,0:T(8,128)(2,1)} %bitcast.4, bf16[96,6144]{1,0:T(8,128)(2,1)} %wout_hbm.1), custom_call_target="tpu_custom_call" | custom-call | flops 1132462080 | bytes 9437184 | tf_op jit(solution)/shard_map/pallas_call | solution.py:390
  77.9 1.3 %copy.11 = bf16[192,24]{0,1:T(8,128)(2,1)} copy(bf16[192,24]{0,1:T(8,128)(2,1)} %bitcast.7) | data formatting | bytes 18432
  79.2 1.9 %copy.12 = f32[1536,96]{0,1:T(8,128)} copy(f32[1536,96]{0,1:T(8,128)} %bitcast.5) | data formatting | bytes 1179648
  81.2 1.9 %copy.13 = f32[96,1536]{1,0:T(8,128)} copy(f32[96,1536]{1,0:T(8,128)} %get-tuple-element.14) | data formatting | bytes 1179648

commit v2 on v1

v2 whole, which is shorter than its diff:
```python
import jax
import jax.numpy as jnp
from jax import lax
from jax.experimental import pallas as pl
from jax.experimental.pallas import tpu as pltpu
from jax.sharding import PartitionSpec as P

F32 = jnp.float32
BF16 = jnp.bfloat16
D = 6144
TOK = 192
HID = 96
LANE = 128
CCOL = D // 8
TPART = TOK // 4
ZCOL = CCOL // 8
PIECE = D // 256
QUART = D // 4
XROWS = 48


def contract_last(left, right):
    return lax.dot_general(left, right, (((1,), (1,)), ((), ())), preferred_element_type=F32)


def remote(src, dst, send, recv, dp, mp):
    return pltpu.make_async_remote_copy(
        src_ref=src,
        dst_ref=dst,
        send_sem=send,
        recv_sem=recv,
        device_id=(dp, mp),
        device_id_type=pl.DeviceIdType.MESH,
    )


def hi_lo(value):
    high = value.astype(BF16).astype(F32)
    return high, (value - high).astype(BF16).astype(F32)


def in_lanes(rows, first, one, two):
    lanes = lax.broadcasted_iota(jnp.int32, (rows, LANE), 1)
    result = jnp.zeros((rows, LANE), F32)
    for k, part in enumerate(hi_lo(one) + hi_lo(two)):
        result = jnp.where(lanes == first + k, part, result)
    return result


def pair_sums(parts):
    return parts[:, 0:1] + parts[:, 1:2], parts[:, 2:3] + parts[:, 3:4]


def kernel(
    x_hbm, go_hbm, gain_ref, win_hbm, wout_hbm,
    gi_ref, gwin_ref, gwout_ref,
    x_v, go_v, g_v, win_v, wout_v, wg, gpg, gain3, pre_s, ga_s, u_s, stat_s, tr_s, gp_t, act_t,
    pair_send, pair_recv, xh_send, xh_recv, gg_s, b_send, b_recv, c_own, c_send, c_recv,
    last_sum, last_send, final, fin_t, fold, unfold,
    x_sem, load_sem, a_send, a_recv, f_send, f_recv, g_send, g_recv, p_send, p_recv,
    h_send, h_recv, bs_sem, br_sem, cs_sem, cr_sem, e_send, e_recv,
):
    dp = lax.axis_index("dp")
    mp = lax.axis_index("mp")
    xh, core = dp // 2, dp % 2
    z, xl, y = mp // 16, (mp // 8) % 2, mp % 8
    zh, zl, yh, yl = z // 2, z % 2, y // 2, y % 2
    cube = 4 * xl + 2 * yl + zl
    pair = 2 * xh + (1 - core)
    far = 2 * (1 - xh) + core

    def place(in_cube, on_y, on_z):
        zp = 2 * on_z + in_cube % 2
        return zp * 16 + (in_cube // 4) * 8 + 2 * on_y + (in_cube // 2) % 2

    def flip(d):
        return (
            4 * ((xl + d // 4) % 2) + 2 * ((yl + (d // 2) % 2) % 2) + (zl + d % 2) % 2
        )

    def cube_mp(d):
        return place(flip(d), yh, zh)

    def y_mp(d):
        return place(cube, (yh + d) % 4, zh)

    def z_mp(d):
        return place(cube, yh, (zh + d) % 8)

    def owner(k):
        return 32 * cube + 4 * zh + k

    def holder(k):
        return place(mp // 32, k, (mp % 32) // 4)

    own_owner = mp // 4 == 8 * cube + zh

    x_loads = [
        pltpu.make_async_copy(
            x_hbm.at[pl.ds(i * XROWS, XROWS)], x_v.at[pl.ds(i * XROWS, XROWS)], x_sem.at[i]
        )
        for i in range(TOK // XROWS)
    ]
    win_load = pltpu.make_async_copy(win_hbm, win_v.at[pl.ds(0, HID)], load_sem.at[0])
    wout_load = pltpu.make_async_copy(wout_hbm, wout_v.at[pl.ds(0, HID)], load_sem.at[1])
    go_load = pltpu.make_async_copy(go_hbm, go_v, load_sem.at[2])
    own_cols = pl.ds(pl.multiple_of(cube * CCOL, CCOL), CCOL)
    own_load = pltpu.make_async_copy(
        win_hbm.at[:, own_cols],
        wg.at[pl.ds(pl.multiple_of(cube * LANE, LANE), HID)],
        load_sem.at[3],
    )
    for load in x_loads:
        load.start()
    win_load.start()
    wout_load.start()
    go_load.start()
    own_load.start()

    barrier = pltpu.get_barrier_semaphore()

    def greet(to_dp, to_mp_):
        pl.semaphore_signal(
            barrier, inc=1, device_id=(to_dp, to_mp_), device_id_type=pl.DeviceIdType.MESH
        )

    @pl.loop(1, 8)
    def _(d):
        greet(dp, cube_mp(d))
        greet(dp, z_mp(d))

    @pl.loop(1, 4)
    def _(d):
        greet(dp, y_mp(d))

    greet(pair, mp)
    greet(far, mp)
    for k in range(4):

        @pl.when(owner(k) != mp)
        def _():
            greet(dp, owner(k))

        @pl.when(holder(k) != mp)
        def _():
            greet(dp, holder(k))

    pl.semaphore_wait(barrier, 7 + 7 + 3 + 2 + jnp.where(own_owner, 6, 8))

    def block_copy(d):
        return remote(
            win_hbm.at[pl.ds(pl.multiple_of(core * 48, 16), 48), pl.ds(pl.multiple_of(flip(d) * CCOL, CCOL), CCOL)],
            wg.at[pl.ds(pl.multiple_of(cube * LANE + core * 48, 16), 48)],
            a_send.at[d], a_recv.at[d], dp, cube_mp(d),
        )

    def landed(d, half):
        return wg.at[pl.ds(pl.multiple_of(flip(d) * LANE + half * 48, 16), 48)]

    def block_arrival(d):
        return remote(
            landed(d, core), landed(d, core), a_send.at[d], a_recv.at[d], dp, cube_mp(d)
        )

    def forward(d):
        return remote(landed(d, core), landed(d, core), f_send.at[d], f_recv.at[d], pair, mp)

    def forward_arrival(d):
        there = landed(d, 1 - core)
        return remote(there, there, f_send.at[d], f_recv.at[d], pair, mp)

    @pl.loop(1, 8)
    def _(d):
        block_copy(d).start()

    for i in range(8):
        wg[i * LANE + HID : (i + 1) * LANE, :] = jnp.zeros((LANE - HID, CCOL), BF16)
    win_v[HID:, :] = jnp.zeros((LANE - HID, D), BF16)
    wout_v[HID:, :] = jnp.zeros((LANE - HID, D), BF16)

    from_lane = lax.broadcasted_iota(jnp.int32, (LANE, LANE), 0)
    to_lane = lax.broadcasted_iota(jnp.int32, (LANE, LANE), 1)
    for g in range(3):
        in_data = jnp.where(to_lane >= 32 * g, jnp.where(to_lane < 32 * g + PIECE, 1.0, 0.0), 0.0)
        in_tail = jnp.where(
            to_lane >= 32 * g + PIECE, jnp.where(to_lane < 32 * g + PIECE + 4, 1.0, 0.0), 0.0
        )
        tail_hit = jnp.where(from_lane == to_lane + (ZCOL - PIECE - 32 * g), in_tail, 0.0)
        for k in range(4):
            hit = jnp.where(from_lane == to_lane + (PIECE * k - 32 * g), in_data, 0.0) + tail_hit
            fold[g * LANE : (g + 1) * LANE, k * LANE : (k + 1) * LANE] = hit.astype(BF16)
    from_row = lax.broadcasted_iota(jnp.int32, (16, 256), 0)
    token = lax.broadcasted_iota(jnp.int32, (16, 256), 1)
    for g in range(3):
        unfold[g, 64:, :] = jnp.zeros((64, 256), BF16)
        for i in range(4):
            unfold[g, i * 16 : (i + 1) * 16, :] = jnp.where(
                token == from_row + (TPART * i + 16 * g), 1.0, 0.0
            ).astype(BF16)

    lane = lax.broadcasted_iota(jnp.int32, (16, LANE), 1)
    for i in range(TOK // XROWS):
        x_loads[i].wait()

        @pl.loop(0, XROWS // 16)
        def _(t):
            rows = pl.ds(pl.multiple_of(i * XROWS + t * 16, 16), 16)
            tile = x_v[rows, :].astype(F32)
            mean = jnp.sum(tile, axis=1, keepdims=True) * (1.0 / D)
            centred = tile - mean
            inv = lax.rsqrt(jnp.sum(centred * centred, axis=1, keepdims=True) * (1.0 / D) + 1e-06)
            g_v[rows, :] = (centred * inv * gain_ref[...]).astype(BF16)
            stat_s[rows, :] = jnp.where(lane < 64, mean, inv)

    gain = gain_ref[...]
    g_hi = gain.astype(BF16).astype(F32)
    g_mid = (gain - g_hi).astype(BF16).astype(F32)
    g_low = gain - g_hi - g_mid
    row = lax.broadcasted_iota(jnp.int32, (16, D), 0)
    gain3[...] = jnp.where(
        row == 0, g_hi, jnp.where(row == 1, g_mid, jnp.where(row == 2, g_low, 0.0))
    ).astype(BF16)

    win_load.wait()
    wout_load.wait()
    go_load.wait()
    pre_s[...] = jnp.zeros_like(pre_s)
    ga_s[...] = jnp.zeros_like(ga_s)
    u_s[...] = jnp.zeros_like(u_s)

    @pl.loop(0, 4)
    def _(k):
        part = pl.ds(pl.multiple_of(k * 1536, 1536), 1536)
        w_part = win_v[:, part]
        pre_s[...] += contract_last(g_v[:, part], w_part)
        u_s[...] += contract_last(gain3[:, part], w_part)
        ga_s[...] += contract_last(go_v[:, part], wout_v[:, part])

    pre = pre_s[...]
    cdf = 0.5 * (1.0 + lax.erf(pre * 0.7071067811865476))
    act = (pre * cdf).astype(BF16).astype(F32)
    slope = cdf + pre * jnp.exp(-0.5 * pre * pre) * 0.3989422804014327
    gp = (ga_s[...] * slope).astype(BF16).astype(F32)
    u_row = jnp.sum(u_s[...], axis=0, keepdims=True)
    sum_one = jnp.sum(gp * u_row, axis=1, keepdims=True)
    sum_two = jnp.sum(gp * pre, axis=1, keepdims=True)
    own_block = pl.ds(pl.multiple_of(cube * LANE, LANE), LANE)
    gpg[:, own_block] = (gp + in_lanes(TOK, HID, sum_one, sum_two)).astype(BF16)

    def gather_copy(d):
        mine = gpg.at[:, own_block]
        return remote(mine, mine, g_send.at[d], g_recv.at[d], dp, cube_mp(d))

    def gather_arrival(d):
        there = gpg.at[:, pl.ds(pl.multiple_of(flip(d) * LANE, LANE), LANE)]
        return remote(there, there, g_send.at[d], g_recv.at[d], dp, cube_mp(d))

    @pl.loop(1, 8)
    def _(d):
        gather_copy(8 - d).start()

    @pl.loop(1, 8)
    def _(d):
        block_arrival(d).wait_recv()
        forward(d).start()

    tr_s[TOK:, :] = jnp.zeros((256 - TOK, LANE), F32)
    for values, target in ((gp, gp_t), (act, act_t)):
        tr_s[:TOK, :] = values
        for b in range(2):
            target[:, b * 128 : (b + 1) * 128] = tr_s[b * 128 : (b + 1) * 128, :].T.astype(BF16)
    sides = ((gp_t, g_v, gwin_ref), (act_t, go_v, gwout_ref))

    def product(side, quarter, t):
        left, right, _ = sides[side]
        cols = pl.ds(pl.multiple_of(quarter * QUART + t * 768, 128), 768)
        return jnp.dot(left[:HID, :TOK], right[:, cols], preferred_element_type=F32)

    def pair_copy(r):
        return remote(pair_send.at[r], pair_recv.at[r], p_send.at[r], p_recv.at[r], pair, mp)

    for r in range(2):
        half = 1 - xh if r == 0 else xh
        for side in range(2):
            for t in range(2):
                pair_send[r, side, :, t * 768 : (t + 1) * 768] = product(
                    side, 2 * half + 1 - core, t
                ).astype(BF16)
        pair_copy(r).start()

    for side in range(2):
        for t in range(2):
            sides[side][2][:, t * 768 : (t + 1) * 768] = product(side, dp, t)

    pair_copy(0).wait_recv()
    for side in range(2):
        for t in range(2):
            cols = slice(t * 768, (t + 1) * 768)
            xh_send[side, :, cols] = (
                product(side, far, t) + pair_recv[0, side, :, cols].astype(F32)
            ).astype(BF16)
    far_copy = remote(xh_send, xh_recv, h_send, h_recv, far, mp)
    far_copy.start()

    own_load.wait()

    @pl.loop(1, 8)
    def _(d):
        gather_arrival(d).wait_recv()
        forward_arrival(d).wait_recv()

    packed = jnp.zeros((TOK, LANE), F32)
    for i in range(8):
        packed += gpg[:, i * LANE : (i + 1) * LANE].astype(F32)
    gg_s[:, CCOL:] = in_lanes(TOK, 0, *pair_sums(packed[:, HID : HID + 4]))
    gg_s[:, :CCOL] = jnp.dot(gpg[...], wg[...], preferred_element_type=F32)

    def token_rows(d):
        return pl.ds(pl.multiple_of((yh + d) % 4 * TPART, 16), TPART)

    def token_copy(d):
        return remote(b_send.at[d], b_recv.at[d], bs_sem.at[d], br_sem.at[d], dp, y_mp(d))

    for d in (2, 1, 3):
        b_send[d] = gg_s[token_rows(d), :].astype(BF16)
        token_copy(d).start()

    part = gg_s[token_rows(0), :]
    for d in range(1, 4):
        token_copy(d).wait_recv()
        part += b_recv[d].astype(F32)

    lanes = lax.broadcasted_iota(jnp.int32, (TPART, LANE), 1)
    tail = in_lanes(TPART, ZCOL, *pair_sums(part[:, CCOL : CCOL + 4]))
    for k in range(8):
        piece = jnp.where(lanes < ZCOL, part[:, k * ZCOL : k * ZCOL + LANE], tail)
        c_own[k] = piece
        c_send[k] = piece.astype(BF16)

    def column_copy(d):
        return remote(
            c_send.at[(zh + d) % 8], c_recv.at[d], cs_sem.at[d], cr_sem.at[d], dp, z_mp(d)
        )

    far_first = (4, 3, 5, 2, 6, 1, 7)
    for d in far_first:
        column_copy(d).start()

    last_sum[...] = c_own[zh]
    for d in far_first:
        column_copy(d).wait_recv()
        last_sum[...] += c_recv[d].astype(F32)

    summed = last_sum[...]
    tail = in_lanes(TPART, ZCOL, *pair_sums(summed[:, ZCOL : ZCOL + 4]))
    rounded = jnp.where(lanes < ZCOL, summed, tail).astype(BF16)
    folded = jnp.dot(
        jnp.concatenate([rounded[16 * g : 16 * (g + 1)] for g in range(3)], axis=1),
        fold[...],
        preferred_element_type=F32,
    ).astype(BF16)
    for k in range(4):
        last_send[k] = folded[:, k * LANE : (k + 1) * LANE]

    def last_copy(k):
        return remote(
            last_send.at[k], final.at[yh], e_send.at[k], e_recv.at[yh], dp, owner(k)
        )

    def last_arrival(k):
        return remote(final.at[k], final.at[k], e_send.at[k], e_recv.at[k], dp, holder(k))

    for k in range(4):

        @pl.when(owner(k) != mp)
        def _():
            last_copy(k).start()

    @pl.when(own_owner)
    def _():
        final[yh] = last_send[mp % 4]

    pair_copy(1).wait_recv()
    far_copy.wait_recv()
    for side in range(2):
        out = sides[side][2]
        out[...] += pair_recv[1, side].astype(F32) + xh_recv[side].astype(F32)

    base = pl.multiple_of(jnp.minimum((mp * PIECE) // 128 * 128, D - 256), 128)
    off = mp * PIECE - base
    span = pl.ds(base, 256)
    picks = lax.broadcasted_iota(jnp.int32, (32, 256), 1) == (
        lax.broadcasted_iota(jnp.int32, (32, 256), 0) + off
    )
    pick = jnp.where(picks, 1.0, 0.0)
    x_t = contract_last(pick.astype(BF16), x_v[:, span])[:PIECE]
    go_t = contract_last(pick.astype(BF16), go_v[:, span])[:PIECE]
    gain_t = jnp.sum(pick * gain_ref[:, span], axis=1, keepdims=True)[:PIECE]
    stat_s[TOK:, :] = jnp.zeros((256 - TOK, LANE), F32)
    for b in range(2):
        fin_t[:, b * 128 : (b + 1) * 128] = stat_s[b * 128 : (b + 1) * 128, :].T
    mean_row, inv_row = fin_t[0:1, :TOK], fin_t[64:65, :TOK]
    normed = (x_t - mean_row) * inv_row

    for k in range(4):

        @pl.when(holder(k) != mp)
        def _():
            last_arrival(k).wait_recv()

    tr_s[64:128, :] = jnp.zeros((64, LANE), F32)
    for i in range(4):
        tr_s[i * 16 : (i + 1) * 16, :] = final[i].astype(F32)
    turned = tr_s[:128, :].T.astype(BF16)
    laid = jnp.zeros((32, 256), F32)
    for g in range(3):
        laid += jnp.dot(turned[32 * g : 32 * (g + 1)], unfold[g], preferred_element_type=F32)
    laid = laid[:, :TOK]
    grad_normed = laid[:PIECE] * gain_t
    mean_one = (laid[PIECE : PIECE + 1] + laid[PIECE + 1 : PIECE + 2]) * (1.0 / D)
    mean_two = (laid[PIECE + 2 : PIECE + 3] + laid[PIECE + 3 : PIECE + 4]) * (1.0 / D)
    gi_ref[...] = (go_t + inv_row * (grad_normed - mean_one - normed * mean_two)).astype(BF16)

    @pl.loop(1, 8)
    def _(d):
        block_copy(d).wait_send()
        forward(d).wait_send()
        gather_copy(d).wait_send()
        column_copy(d).wait_send()

    for r in range(2):
        pair_copy(r).wait_send()
    far_copy.wait_send()

    @pl.loop(1, 4)
    def _(d):
        token_copy(d).wait_send()

    for k in range(4):

        @pl.when(owner(k) != mp)
        def _():
            last_copy(k).wait_send()


def place_outputs(gi, gwin, gwout, gi_out, gwin_out, gwout_out, gi_v, w_v, in_sem, out_sem):
    parts = [(gi, gi_v, gi_out)]
    for side, (array, out) in enumerate(((gwin, gwin_out), (gwout, gwout_out))):
        for k in range(4):
            rows = pl.ds(k * 24, 24)
            parts.append((array.at[rows], w_v.at[side, rows], out.at[rows]))
    reads, writes = [], []
    for k, (array, held, out) in enumerate(parts):
        reads.append(pltpu.make_async_copy(array, held, in_sem.at[k]))
        writes.append(pltpu.make_async_copy(held, out, out_sem.at[k]))
    for read in reads:
        read.start()
    for read, write in zip(reads, writes):
        read.wait()
        write.start()
    for write in writes:
        write.wait()


def shards(block_input, grad_out, ln_gain, w_in, w_out):
    dma = pltpu.SemaphoreType.DMA
    grad_input, grad_w_in, grad_w_out = pl.pallas_call(
        kernel,
        out_shape=(
            jax.ShapeDtypeStruct((PIECE, TOK), BF16),
            jax.ShapeDtypeStruct((HID, QUART), F32),
            jax.ShapeDtypeStruct((HID, QUART), F32),
        ),
        in_specs=[
            pl.BlockSpec(memory_space=pl.ANY),
            pl.BlockSpec(memory_space=pl.ANY),
            pl.BlockSpec(memory_space=pltpu.VMEM),
            pl.BlockSpec(memory_space=pl.ANY),
            pl.BlockSpec(memory_space=pl.ANY),
        ],
        out_specs=[pl.BlockSpec(memory_space=pltpu.VMEM)] * 3,
        scratch_shapes=[
            pltpu.VMEM((TOK, D), BF16),
            pltpu.VMEM((TOK, D), BF16),
            pltpu.VMEM((TOK, D), BF16),
            pltpu.VMEM((LANE, D), BF16),
            pltpu.VMEM((LANE, D), BF16),
            pltpu.VMEM((8 * LANE, CCOL), BF16),
            pltpu.VMEM((TOK, 8 * LANE), BF16),
            pltpu.VMEM((16, D), BF16),
            pltpu.VMEM((TOK, LANE), F32),
            pltpu.VMEM((TOK, LANE), F32),
            pltpu.VMEM((16, LANE), F32),
            pltpu.VMEM((256, LANE), F32),
            pltpu.VMEM((256, LANE), F32),
            pltpu.VMEM((LANE, 256), BF16),
            pltpu.VMEM((LANE, 256), BF16),
            pltpu.VMEM((2, 2, HID, QUART), BF16),
            pltpu.VMEM((2, 2, HID, QUART), BF16),
            pltpu.VMEM((2, HID, QUART), BF16),
            pltpu.VMEM((2, HID, QUART), BF16),
            pltpu.VMEM((TOK, CCOL + LANE), F32),
            pltpu.VMEM((4, TPART, CCOL + LANE), BF16),
            pltpu.VMEM((4, TPART, CCOL + LANE), BF16),
            pltpu.VMEM((8, TPART, LANE), F32),
            pltpu.VMEM((8, TPART, LANE), BF16),
            pltpu.VMEM((8, TPART, LANE), BF16),
            pltpu.VMEM((TPART, LANE), F32),
            pltpu.VMEM((4, 16, LANE), BF16),
            pltpu.VMEM((4, 16, LANE), BF16),
            pltpu.VMEM((LANE, 256), F32),
            pltpu.VMEM((3 * LANE, 4 * LANE), BF16),
            pltpu.VMEM((3, LANE, 256), BF16),
            dma((4,)), dma((4,)),
            dma((8,)), dma((8,)), dma((8,)), dma((8,)), dma((8,)), dma((8,)),
            dma((2,)), dma((2,)), dma, dma,
            dma((4,)), dma((4,)), dma((8,)), dma((8,)), dma((4,)), dma((4,)),
        ],
        compiler_params=pltpu.CompilerParams(
            collective_id=0, has_side_effects=True, vmem_limit_bytes=60 * 1024 * 1024
        ),
        cost_estimate=pl.CostEstimate(
            flops=2 * 5 * TOK * D * HID, bytes_accessed=9 * 1024 * 1024, transcendentals=TOK * HID
        ),
    )(block_input, grad_out, ln_gain.reshape(1, D), w_in.T, w_out)
    grad_input, grad_w_in, grad_w_out = pl.pallas_call(
        place_outputs,
        out_shape=(
            jax.ShapeDtypeStruct((PIECE, TOK), BF16),
            jax.ShapeDtypeStruct((HID, QUART), F32),
            jax.ShapeDtypeStruct((HID, QUART), F32),
        ),
        in_specs=[pl.BlockSpec(memory_space=pl.ANY)] * 3,
        out_specs=[pl.BlockSpec(memory_space=pl.ANY)] * 3,
        scratch_shapes=[
            pltpu.VMEM((PIECE, TOK), BF16),
            pltpu.VMEM((2, HID, QUART), F32),
            dma((9,)),
            dma((9,)),
        ],
        compiler_params=pltpu.CompilerParams(vmem_limit_bytes=60 * 1024 * 1024),
    )(grad_input, grad_w_in, grad_w_out)
    return grad_input.T, grad_w_in.T, grad_w_out


def solution(mesh):
    in_specs = (P("dp", None), P("dp", None), P(), P(None, "mp"), P("mp", None))
    out_specs = (P("dp", "mp"), P("dp", "mp"), P("mp", "dp"))
    return jax.shard_map(shards, mesh=mesh, in_specs=in_specs, out_specs=out_specs, check_vma=False)
```

time: 83.4 us -> 68.9 us (0.83)
  the two profiles are of different devices: /device:TPU:22 before, /device:TPU:68 now
where the time goes in v2:
time: 68.9 us; the launch traced here: 68.6 us
  Pallas kernels  68 us (99%)
    pallas_call x1, Pallas kernels, shards(): pl.pallas_call(kernel, out_shape=(jax.ShapeDtypeStruct((PIECE, TOK), BF16...  65.8 us
    pallas_call x1, Pallas kernels, shards(): pl.pallas_call(place_outputs, out_shape=(jax.ShapeDtypeStruct((PIECE, TOK...  2.18 us

profile of v2, /device:TPU:68, one launch (start us, length us, event | category | flops | bytes accessed | tf_op | source)
XLA Modules:
  0.0 68.6 jit_solution(14382455685526987878)
XLA Ops:
  0.6 65.8 %shard_map.76 = (bf16[24,192]{1,0:T(8,128)(2,1)}, f32[96,1536]{1,0:T(8,128)}, f32[96,1536]{1,0:T(8,128)}) custom-call(bf16[192,6144]{1,0:T(8,128)(2,1)} %x_hbm.1, bf16[192,6144]{1,0:T(8,128)(2,1)} %go_hbm.1, f32[1,6144]{1,0:T(1,128)} %bitcast.5, bf16[96,6144]{1,0:T(8,128)(2,1)} %bitcast.4, bf16[96,6144]{1,0:T(8,128)(2,1)} %wout_hbm.1), custom_call_target="tpu_custom_call" | custom-call | flops 1132462080 | bytes 9437184 | tf_op jit(solution)/shard_map/pallas_call | solution.py:467
  66.5 2.2 %shard_map.77 = (bf16[24,192]{1,0:T(8,128)(2,1)}, f32[96,1536]{1,0:T(8,128)}, f32[96,1536]{1,0:T(8,128)}) custom-call(bf16[24,192]{1,0:T(8,128)(2,1)} %get-tuple-element.9.gi, f32[96,1536]{1,0:T(8,128)} %get-tuple-element.10.gwin, f32[96,1536]{1,0:T(8,128)} %get-tuple-element.11.gwout), custom_call_target="tpu_custom_call" | custom-call | tf_op jit(solution)/shard_map/pallas_call | solution.py:526

commit v3 on v2

--- a/solution.py
+++ b/solution.py
@@ -56,9 +56,9 @@
     gi_ref, gwin_ref, gwout_ref,
     x_v, go_v, g_v, win_v, wout_v, wg, gpg, gain3, pre_s, ga_s, u_s, stat_s, tr_s, gp_t, act_t,
     pair_send, pair_recv, xh_send, xh_recv, gg_s, b_send, b_recv, c_own, c_send, c_recv,
-    last_sum, last_send, final, fin_t, fold, unfold,
+    o_own, o_send, o_recv, t_own, t_send, t_recv, last_send, final, fin_t, fold, unfold,
     x_sem, load_sem, a_send, a_recv, f_send, f_recv, g_send, g_recv, p_send, p_recv,
-    h_send, h_recv, bs_sem, br_sem, cs_sem, cr_sem, e_send, e_recv,
+    h_send, h_recv, bs_sem, br_sem, cs_sem, cr_sem, os_sem, or_sem, ts_sem, tr_sem, e_send, e_recv,
 ):
     dp = lax.axis_index("dp")
     mp = lax.axis_index("mp")
@@ -173,10 +173,173 @@
     def _(d):
         block_copy(d).start()
 
+    win_v[HID:, :] = jnp.zeros((LANE - HID, D), BF16)
+    wout_v[HID:, :] = jnp.zeros((LANE - HID, D), BF16)
+
+    gain = gain_ref[...]
+    g_hi = gain.astype(BF16).astype(F32)
+    g_mid = (gain - g_hi).astype(BF16).astype(F32)
+    g_low = gain - g_hi - g_mid
+    row = lax.broadcasted_iota(jnp.int32, (16, D), 0)
+    gain3[...] = jnp.where(
+        row == 0, g_hi, jnp.where(row == 1, g_mid, jnp.where(row == 2, g_low, 0.0))
+    ).astype(BF16)
+
+    lane = lax.broadcasted_iota(jnp.int32, (16, LANE), 1)
+
+    def norm_chunk(i):
+        x_loads[i].wait()
+
+        @pl.loop(0, XROWS // 16)
+        def _(t):
+            rows = pl.ds(pl.multiple_of(i * XROWS + t * 16, 16), 16)
+            tile = x_v[rows, :].astype(F32)
+            mean = jnp.sum(tile, axis=1, keepdims=True) * (1.0 / D)
+            centred = tile - mean
+            inv = lax.rsqrt(jnp.sum(centred * centred, axis=1, keepdims=True) * (1.0 / D) + 1e-06)
+            g_v[rows, :] = (centred * inv * gain_ref[...]).astype(BF16)
+            stat_s[rows, :] = jnp.where(lane < 64, mean, inv)
+
+    norm_chunk(0)
+
+    for i in range(1, TOK // XROWS):
+        norm_chunk(i)
+
+    win_load.wait()
+    wout_load.wait()
+    go_load.wait()
+    pre_s[...] = jnp.zeros_like(pre_s)
+    u_s[...] = jnp.zeros_like(u_s)
+    ga_s[...] = jnp.zeros_like(ga_s)
+
+    @pl.loop(0, 4)
+    def _(k):
+        part = pl.ds(pl.multiple_of(k * 1536, 1536), 1536)
+        w_part = win_v[:, part]
+        pre_s[...] += contract_last(g_v[:, part], w_part)
+        u_s[...] += contract_last(gain3[:, part], w_part)
+        ga_s[...] += contract_last(go_v[:, part], wout_v[:, part])
+
+    pre = pre_s[...]
+    cdf = 0.5 * (1.0 + lax.erf(pre * 0.7071067811865476))
+    act = (pre * cdf).astype(BF16).astype(F32)
+    slope = cdf + pre * jnp.exp(-0.5 * pre * pre) * 0.3989422804014327
+    gp = (ga_s[...] * slope).astype(BF16).astype(F32)
+    u_row = jnp.sum(u_s[...], axis=0, keepdims=True)
+    sum_one = jnp.sum(gp * u_row, axis=1, keepdims=True)
+    sum_two = jnp.sum(gp * pre, axis=1, keepdims=True)
+    own_block = pl.ds(pl.multiple_of(cube * LANE, LANE), LANE)
+    gpg[:, own_block] = (gp + in_lanes(TOK, HID, sum_one, sum_two)).astype(BF16)
+
+    def gather_copy(d):
+        mine = gpg.at[:, own_block]
+        return remote(mine, mine, g_send.at[d], g_recv.at[d], dp, cube_mp(d))
+
+    def gather_arrival(d):
+        there = gpg.at[:, pl.ds(pl.multiple_of(flip(d) * LANE, LANE), LANE)]
+        return remote(there, there, g_send.at[d], g_recv.at[d], dp, cube_mp(d))
+
+    @pl.loop(1, 8)
+    def _(d):
+        gather_copy(8 - d).start()
+
+    @pl.loop(1, 8)
+    def _(d):
+        block_arrival(d).wait_recv()
+        forward(d).start()
+
     for i in range(8):
         wg[i * LANE + HID : (i + 1) * LANE, :] = jnp.zeros((LANE - HID, CCOL), BF16)
-    win_v[HID:, :] = jnp.zeros((LANE - HID, D), BF16)
-    wout_v[HID:, :] = jnp.zeros((LANE - HID, D), BF16)
+
+    tr_s[TOK:, :] = jnp.zeros((256 - TOK, LANE), F32)
+    for values, target in ((gp, gp_t), (act, act_t)):
+        tr_s[:TOK, :] = values
+        for b in range(2):
+            target[:, b * 128 : (b + 1) * 128] = tr_s[b * 128 : (b + 1) * 128, :].T.astype(BF16)
+    sides = ((gp_t, g_v, gwin_ref), (act_t, go_v, gwout_ref))
+
+    def product(side, quarter, t):
+        left, right, _ = sides[side]
+        cols = pl.ds(pl.multiple_of(quarter * QUART + t * 768, 128), 768)
+        return jnp.dot(left[:HID, :TOK], right[:, cols], preferred_element_type=F32)
+
+    def pair_copy(r):
+        return remote(pair_send.at[r], pair_recv.at[r], p_send.at[r], p_recv.at[r], pair, mp)
+
+    for r in range(2):
+        half = 1 - xh if r == 0 else xh
+        for side in range(2):
+            for t in range(2):
+                pair_send[r, side, :, t * 768 : (t + 1) * 768] = product(
+                    side, 2 * half + 1 - core, t
+                ).astype(BF16)
+        pair_copy(r).start()
+
+    for side in range(2):
+        for t in range(2):
+            sides[side][2][:, t * 768 : (t + 1) * 768] = product(side, dp, t)
+
+    pair_copy(0).wait_recv()
+    for side in range(2):
+        for t in range(2):
+            cols = slice(t * 768, (t + 1) * 768)
+            xh_send[side, :, cols] = (
+                product(side, far, t) + pair_recv[0, side, :, cols].astype(F32)
+            ).astype(BF16)
+    far_copy = remote(xh_send, xh_recv, h_send, h_recv, far, mp)
+    far_copy.start()
+
+    own_load.wait()
+
+    @pl.loop(1, 8)
+    def _(d):
+        gather_arrival(d).wait_recv()
+        forward_arrival(d).wait_recv()
+
+    packed = jnp.zeros((TOK, LANE), F32)
+    for i in range(8):
+        packed += gpg[:, i * LANE : (i + 1) * LANE].astype(F32)
+    gg_s[:, CCOL:] = in_lanes(TOK, 0, *pair_sums(packed[:, HID : HID + 4]))
+    gg_s[:, :CCOL] = jnp.dot(gpg[...], wg[...], preferred_element_type=F32)
+
+    far_first = (4, 3, 5, 2, 6, 1, 7)
+
+    def pieces(values, own, send):
+        rows = values.shape[0]
+        lanes = lax.broadcasted_iota(jnp.int32, (rows, LANE), 1)
+        tail = in_lanes(rows, ZCOL, *pair_sums(values[:, CCOL : CCOL + 4]))
+        for k in range(8):
+            piece = jnp.where(lanes < ZCOL, values[:, k * ZCOL : k * ZCOL + LANE], tail)
+            own[k] = piece
+            send[k] = piece.astype(BF16)
+
+    def token_rows(d):
+        return pl.ds(pl.multiple_of((yh + d) % 4 * 32, 32), 32)
+
+    def token_copy(d):
+        return remote(b_send.at[d], b_recv.at[d], bs_sem.at[d], br_sem.at[d], dp, y_mp(d))
+
+    def column_copy(d):
+        return remote(
+            c_send.at[(zh + d) % 8], c_recv.at[d], cs_sem.at[d], cr_sem.at[d], dp, z_mp(d)
+        )
+
+    def other_column_copy(d):
+        return remote(
+            o_send.at[(zh + d) % 8], o_recv.at[d], os_sem.at[d], or_sem.at[d], dp, z_mp(d)
+        )
+
+    def other_token_copy(d):
+        return remote(
+            t_send.at[(yh + d) % 4], t_recv.at[d], ts_sem.at[d], tr_sem.at[d], dp, y_mp(d)
+        )
+
+    for d in (2, 1, 3):
+        b_send[d] = gg_s[token_rows(d), :].astype(BF16)
+        token_copy(d).start()
+    pieces(gg_s[128:, :], o_own, o_send)
+    for d in far_first:
+        other_column_copy(d).start()
 
     from_lane = lax.broadcasted_iota(jnp.int32, (LANE, LANE), 0)
     to_lane = lax.broadcasted_iota(jnp.int32, (LANE, LANE), 1)
@@ -195,163 +358,41 @@
         unfold[g, 64:, :] = jnp.zeros((64, 256), BF16)
         for i in range(4):
             unfold[g, i * 16 : (i + 1) * 16, :] = jnp.where(
-                token == from_row + (TPART * i + 16 * g), 1.0, 0.0
+                token == from_row + (32 * i + 16 * g if g < 2 else 128 + 16 * i), 1.0, 0.0
             ).astype(BF16)
 
-    lane = lax.broadcasted_iota(jnp.int32, (16, LANE), 1)
-    for i in range(TOK // XROWS):
-        x_loads[i].wait()
-
-        @pl.loop(0, XROWS // 16)
-        def _(t):
-            rows = pl.ds(pl.multiple_of(i * XROWS + t * 16, 16), 16)
-            tile = x_v[rows, :].astype(F32)
-            mean = jnp.sum(tile, axis=1, keepdims=True) * (1.0 / D)
-            centred = tile - mean
-            inv = lax.rsqrt(jnp.sum(centred * centred, axis=1, keepdims=True) * (1.0 / D) + 1e-06)
-            g_v[rows, :] = (centred * inv * gain_ref[...]).astype(BF16)
-            stat_s[rows, :] = jnp.where(lane < 64, mean, inv)
-
-    gain = gain_ref[...]
-    g_hi = gain.astype(BF16).astype(F32)
-    g_mid = (gain - g_hi).astype(BF16).astype(F32)
-    g_low = gain - g_hi - g_mid
-    row = lax.broadcasted_iota(jnp.int32, (16, D), 0)
-    gain3[...] = jnp.where(
-        row == 0, g_hi, jnp.where(row == 1, g_mid, jnp.where(row == 2, g_low, 0.0))
-    ).astype(BF16)
-
-    win_load.wait()
-    wout_load.wait()
-    go_load.wait()
-    pre_s[...] = jnp.zeros_like(pre_s)
-    ga_s[...] = jnp.zeros_like(ga_s)
-    u_s[...] = jnp.zeros_like(u_s)
-
-    @pl.loop(0, 4)
-    def _(k):
-        part = pl.ds(pl.multiple_of(k * 1536, 1536), 1536)
-        w_part = win_v[:, part]
-        pre_s[...] += contract_last(g_v[:, part], w_part)
-        u_s[...] += contract_last(gain3[:, part], w_part)
-        ga_s[...] += contract_last(go_v[:, part], wout_v[:, part])
-
-    pre = pre_s[...]
-    cdf = 0.5 * (1.0 + lax.erf(pre * 0.7071067811865476))
-    act = (pre * cdf).astype(BF16).astype(F32)
-    slope = cdf + pre * jnp.exp(-0.5 * pre * pre) * 0.3989422804014327
-    gp = (ga_s[...] * slope).astype(BF16).astype(F32)
-    u_row = jnp.sum(u_s[...], axis=0, keepdims=True)
-    sum_one = jnp.sum(gp * u_row, axis=1, keepdims=True)
-    sum_two = jnp.sum(gp * pre, axis=1, keepdims=True)
-    own_block = pl.ds(pl.multiple_of(cube * LANE, LANE), LANE)
-    gpg[:, own_block] = (gp + in_lanes(TOK, HID, sum_one, sum_two)).astype(BF16)
-
-    def gather_copy(d):
-        mine = gpg.at[:, own_block]
-        return remote(mine, mine, g_send.at[d], g_recv.at[d], dp, cube_mp(d))
-
-    def gather_arrival(d):
-        there = gpg.at[:, pl.ds(pl.multiple_of(flip(d) * LANE, LANE), LANE)]
-        return remote(there, there, g_send.at[d], g_recv.at[d], dp, cube_mp(d))
-
-    @pl.loop(1, 8)
-    def _(d):
-        gather_copy(8 - d).start()
-
-    @pl.loop(1, 8)
-    def _(d):
-        block_arrival(d).wait_recv()
-        forward(d).start()
-
-    tr_s[TOK:, :] = jnp.zeros((256 - TOK, LANE), F32)
-    for values, target in ((gp, gp_t), (act, act_t)):
-        tr_s[:TOK, :] = values
-        for b in range(2):
-            target[:, b * 128 : (b + 1) * 128] = tr_s[b * 128 : (b + 1) * 128, :].T.astype(BF16)
-    sides = ((gp_t, g_v, gwin_ref), (act_t, go_v, gwout_ref))
-
-    def product(side, quarter, t):
-        left, right, _ = sides[side]
-        cols = pl.ds(pl.multiple_of(quarter * QUART + t * 768, 128), 768)
-        return jnp.dot(left[:HID, :TOK], right[:, cols], preferred_element_type=F32)
-
-    def pair_copy(r):
-        return remote(pair_send.at[r], pair_recv.at[r], p_send.at[r], p_recv.at[r], pair, mp)
-
-    for r in range(2):
-        half = 1 - xh if r == 0 else xh
-        for side in range(2):
-            for t in range(2):
-                pair_send[r, side, :, t * 768 : (t + 1) * 768] = product(
-                    side, 2 * half + 1 - core, t
-                ).astype(BF16)
-        pair_copy(r).start()
-
-    for side in range(2):
-        for t in range(2):
-            sides[side][2][:, t * 768 : (t + 1) * 768] = product(side, dp, t)
-
-    pair_copy(0).wait_recv()
-    for side in range(2):
-        for t in range(2):
-            cols = slice(t * 768, (t + 1) * 768)
-            xh_send[side, :, cols] = (
-                product(side, far, t) + pair_recv[0, side, :, cols].astype(F32)
-            ).astype(BF16)
-    far_copy = remote(xh_send, xh_recv, h_send, h_recv, far, mp)
-    far_copy.start()
-
-    own_load.wait()
-
-    @pl.loop(1, 8)
-    def _(d):
-        gather_arrival(d).wait_recv()
-        forward_arrival(d).wait_recv()
-
-    packed = jnp.zeros((TOK, LANE), F32)
-    for i in range(8):
-        packed += gpg[:, i * LANE : (i + 1) * LANE].astype(F32)
-    gg_s[:, CCOL:] = in_lanes(TOK, 0, *pair_sums(packed[:, HID : HID + 4]))
-    gg_s[:, :CCOL] = jnp.dot(gpg[...], wg[...], preferred_element_type=F32)
-
-    def token_rows(d):
-        return pl.ds(pl.multiple_of((yh + d) % 4 * TPART, 16), TPART)
-
-    def token_copy(d):
-        return remote(b_send.at[d], b_recv.at[d], bs_sem.at[d], br_sem.at[d], dp, y_mp(d))
-
-    for d in (2, 1, 3):
-        b_send[d] = gg_s[token_rows(d), :].astype(BF16)
-        token_copy(d).start()
-
     part = gg_s[token_rows(0), :]
-    for d in range(1, 4):
+    for d in (1, 3, 2):
         token_copy(d).wait_recv()
         part += b_recv[d].astype(F32)
-
-    lanes = lax.broadcasted_iota(jnp.int32, (TPART, LANE), 1)
-    tail = in_lanes(TPART, ZCOL, *pair_sums(part[:, CCOL : CCOL + 4]))
-    for k in range(8):
-        piece = jnp.where(lanes < ZCOL, part[:, k * ZCOL : k * ZCOL + LANE], tail)
-        c_own[k] = piece
-        c_send[k] = piece.astype(BF16)
-
-    def column_copy(d):
-        return remote(
-            c_send.at[(zh + d) % 8], c_recv.at[d], cs_sem.at[d], cr_sem.at[d], dp, z_mp(d)
-        )
-
-    far_first = (4, 3, 5, 2, 6, 1, 7)
+    pieces(part, c_own, c_send)
     for d in far_first:
         column_copy(d).start()
 
-    last_sum[...] = c_own[zh]
-    for d in far_first:
+    o_sum = o_own[zh]
+    for d in (1, 7, 2, 6, 3, 5, 4):
+        other_column_copy(d).wait_recv()
+        o_sum += o_recv[d].astype(F32)
+    lanes = lax.broadcasted_iota(jnp.int32, (64, LANE), 1)
+    tail = in_lanes(64, ZCOL, *pair_sums(o_sum[:, ZCOL : ZCOL + 4]))
+    o_sum = jnp.where(lanes < ZCOL, o_sum, tail)
+    for k in range(4):
+        t_own[k] = o_sum[16 * k : 16 * (k + 1)]
+        t_send[k] = t_own[k].astype(BF16)
+    for d in (2, 1, 3):
+        other_token_copy(d).start()
+
+    c_sum = c_own[zh]
+    for d in (1, 7, 2, 6, 3, 5, 4):
         column_copy(d).wait_recv()
-        last_sum[...] += c_recv[d].astype(F32)
-
-    summed = last_sum[...]
+        c_sum += c_recv[d].astype(F32)
+    t_sum = t_own[yh]
+    for d in (1, 3, 2):
+        other_token_copy(d).wait_recv()
+        t_sum += t_recv[d].astype(F32)
+
+    lanes = lax.broadcasted_iota(jnp.int32, (TPART, LANE), 1)
+    summed = jnp.concatenate([c_sum, t_sum], axis=0)
     tail = in_lanes(TPART, ZCOL, *pair_sums(summed[:, ZCOL : ZCOL + 4]))
     rounded = jnp.where(lanes < ZCOL, summed, tail).astype(BF16)
     folded = jnp.dot(
@@ -427,6 +468,7 @@
         forward(d).wait_send()
         gather_copy(d).wait_send()
         column_copy(d).wait_send()
+        other_column_copy(d).wait_send()
 
     for r in range(2):
         pair_copy(r).wait_send()
@@ -435,6 +477,7 @@
     @pl.loop(1, 4)
     def _(d):
         token_copy(d).wait_send()
+        other_token_copy(d).wait_send()
 
     for k in range(4):
 
@@ -500,12 +543,17 @@
             pltpu.VMEM((2, HID, QUART), BF16),
             pltpu.VMEM((2, HID, QUART), BF16),
             pltpu.VMEM((TOK, CCOL + LANE), F32),
-            pltpu.VMEM((4, TPART, CCOL + LANE), BF16),
-            pltpu.VMEM((4, TPART, CCOL + LANE), BF16),
-            pltpu.VMEM((8, TPART, LANE), F32),
-            pltpu.VMEM((8, TPART, LANE), BF16),
-            pltpu.VMEM((8, TPART, LANE), BF16),
-            pltpu.VMEM((TPART, LANE), F32),
+            pltpu.VMEM((4, 32, CCOL + LANE), BF16),
+            pltpu.VMEM((4, 32, CCOL + LANE), BF16),
+            pltpu.VMEM((8, 32, LANE), F32),
+            pltpu.VMEM((8, 32, LANE), BF16),
+            pltpu.VMEM((8, 32, LANE), BF16),
+            pltpu.VMEM((8, 64, LANE), F32),
+            pltpu.VMEM((8, 64, LANE), BF16),
+            pltpu.VMEM((8, 64, LANE), BF16),
+            pltpu.VMEM((4, 16, LANE), F32),
+            pltpu.VMEM((4, 16, LANE), BF16),
+            pltpu.VMEM((4, 16, LANE), BF16),
             pltpu.VMEM((4, 16, LANE), BF16),
             pltpu.VMEM((4, 16, LANE), BF16),
             pltpu.VMEM((LANE, 256), F32),
@@ -514,7 +562,8 @@
             dma((4,)), dma((4,)),
             dma((8,)), dma((8,)), dma((8,)), dma((8,)), dma((8,)), dma((8,)),
             dma((2,)), dma((2,)), dma, dma,
-            dma((4,)), dma((4,)), dma((8,)), dma((8,)), dma((4,)), dma((4,)),
+            dma((4,)), dma((4,)), dma((8,)), dma((8,)), dma((8,)), dma((8,)), dma((4,)), dma((4,)),
+            dma((4,)), dma((4,)),
         ],
         compiler_params=pltpu.CompilerParams(
             collective_id=0, has_side_effects=True, vmem_limit_bytes=60 * 1024 * 1024

time: 68.9 us -> 66.7 us (0.968)
  the two profiles are of different devices: /device:TPU:68 before, /device:TPU:64 now
where the time goes in v3:
time: 66.7 us; the launch traced here: 66.5 us
  Pallas kernels  65.8 us (99%)
    pallas_call x1, Pallas kernels, shards(): pl.pallas_call(kernel, out_shape=(jax.ShapeDtypeStruct((PIECE, TOK), BF16...  63.7 us
    pallas_call x1, Pallas kernels, shards(): pl.pallas_call(place_outputs, out_shape=(jax.ShapeDtypeStruct((PIECE, TOK...  2.18 us

profile of v3, /device:TPU:64, one launch (start us, length us, event | category | flops | bytes accessed | tf_op | source)
XLA Modules:
  0.0 66.5 jit_solution(1697999413626029903)
XLA Ops:
  0.6 63.7 %shard_map.76 = (bf16[24,192]{1,0:T(8,128)(2,1)}, f32[96,1536]{1,0:T(8,128)}, f32[96,1536]{1,0:T(8,128)}) custom-call(bf16[192,6144]{1,0:T(8,128)(2,1)} %x_hbm.1, bf16[192,6144]{1,0:T(8,128)(2,1)} %go_hbm.1, f32[1,6144]{1,0:T(1,128)} %bitcast.5, bf16[96,6144]{1,0:T(8,128)(2,1)} %bitcast.4, bf16[96,6144]{1,0:T(8,128)(2,1)} %wout_hbm.1), custom_call_target="tpu_custom_call" | custom-call | flops 1132462080 | bytes 9437184 | tf_op jit(solution)/shard_map/pallas_call | solution.py:510
  64.3 2.2 %shard_map.77 = (bf16[24,192]{1,0:T(8,128)(2,1)}, f32[96,1536]{1,0:T(8,128)}, f32[96,1536]{1,0:T(8,128)}) custom-call(bf16[24,192]{1,0:T(8,128)(2,1)} %get-tuple-element.9.gi, f32[96,1536]{1,0:T(8,128)} %get-tuple-element.10.gwin, f32[96,1536]{1,0:T(8,128)} %get-tuple-element.11.gwout), custom_call_target="tpu_custom_call" | custom-call | tf_op jit(solution)/shard_map/pallas_call | solution.py:575

commit v4 on v3

--- a/solution.py
+++ b/solution.py
@@ -171,7 +171,7 @@
 
     @pl.loop(1, 8)
     def _(d):
-        block_copy(d).start()
+        block_copy(8 - d).start()
 
     win_v[HID:, :] = jnp.zeros((LANE - HID, D), BF16)
     wout_v[HID:, :] = jnp.zeros((LANE - HID, D), BF16)
@@ -245,8 +245,8 @@
 
     @pl.loop(1, 8)
     def _(d):
-        block_arrival(d).wait_recv()
-        forward(d).start()
+        block_arrival(8 - d).wait_recv()
+        forward(8 - d).start()
 
     for i in range(8):
         wg[i * LANE + HID : (i + 1) * LANE, :] = jnp.zeros((LANE - HID, CCOL), BF16)

time: 66.7 us -> 64.1 us (0.961)
  the two profiles are of different devices: /device:TPU:64 before, /device:TPU:68 now
where the time goes in v4:
time: 64.1 us; the launch traced here: 63.8 us
  Pallas kernels  63.2 us (99%)
    pallas_call x1, Pallas kernels, shards(): pl.pallas_call(kernel, out_shape=(jax.ShapeDtypeStruct((PIECE, TOK), BF16...  61 us
    pallas_call x1, Pallas kernels, shards(): pl.pallas_call(place_outputs, out_shape=(jax.ShapeDtypeStruct((PIECE, TOK...  2.18 us

profile of v4, /device:TPU:68, one launch (start us, length us, event | category | flops | bytes accessed | tf_op | source)
XLA Modules:
  0.0 63.8 jit_solution(12050434274731075081)
XLA Ops:
  0.6 61.0 %shard_map.76 = (bf16[24,192]{1,0:T(8,128)(2,1)}, f32[96,1536]{1,0:T(8,128)}, f32[96,1536]{1,0:T(8,128)}) custom-call(bf16[192,6144]{1,0:T(8,128)(2,1)} %x_hbm.1, bf16[192,6144]{1,0:T(8,128)(2,1)} %go_hbm.1, f32[1,6144]{1,0:T(1,128)} %bitcast.5, bf16[96,6144]{1,0:T(8,128)(2,1)} %bitcast.4, bf16[96,6144]{1,0:T(8,128)(2,1)} %wout_hbm.1), custom_call_target="tpu_custom_call" | custom-call | flops 1132462080 | bytes 9437184 | tf_op jit(solution)/shard_map/pallas_call | solution.py:510
  61.6 2.2 %shard_map.77 = (bf16[24,192]{1,0:T(8,128)(2,1)}, f32[96,1536]{1,0:T(8,128)}, f32[96,1536]{1,0:T(8,128)}) custom-call(bf16[24,192]{1,0:T(8,128)(2,1)} %get-tuple-element.9.gi, f32[96,1536]{1,0:T(8,128)} %get-tuple-element.10.gwin, f32[96,1536]{1,0:T(8,128)} %get-tuple-element.11.gwout), custom_call_target="tpu_custom_call" | custom-call | tf_op jit(solution)/shard_map/pallas_call | solution.py:575
